TPU v7x, 32 devices: a whole 2x2x4 slice. The times are simulated.
32 devices in a mesh: groups: 2 (over y), inst: 8 (over z, x), tp: 2 (over core).
Axes of the slice: x: 2, y: 2, z: 4, core: 2. Of those that a mesh axis runs over, the one named last changes fastest.
Arguments:
- source_cache: bfloat16 [16, 6, 4, 2, 128, 128], P(('groups', 'inst'), None, None, None, 'tp'), parts along dimension 0, may hold values from -18 to 18
- block_table: int32 [16, 6], P(('groups', 'inst')), parts along dimension 0, may hold values from 0 to 5, each once within a row
- lengths: int32 [16, 6], P('groups'), parts along dimension 0, may hold values from 16 to 128, as said below
- target_map: int32 [16, 6], P('groups'), parts along dimension 0, may hold values from 0 to 7, as said below
- queries: bfloat16 [6, 16, 6, 64, 128], P(None, ('groups', 'inst'), None, 'tp'), parts along dimension 1, may hold values from -50 to 50
- fresh_cache: bfloat16 [6, 16, 6, 4, 2, 128], P(None, ('groups', 'inst'), None, 'tp'), parts along dimension 1, may hold values from -6 to 6
- positions: int32 [16, 6], P(('groups', 'inst')), parts along dimension 0, may hold values from 256 to 4095
Outputs:
- scales: bfloat16 [16, 6, 4, 2], P(('groups', 'inst'), None, 'tp'), parts along dimension 0
- attended: bfloat16 [6, 16, 6, 64, 128], P(None, ('groups', 'inst'), None, 'tp'), parts along dimension 1
There are 2 independent parts, one for each index of `groups`. A program takes and returns all parts, laid end to end along the dimension named above; each array names one. Nothing has to cross between parts.
Inputs may be any that keep to these rules, and one draw needn't show every extreme that they name: `target_map`: for each request number j the sources go to distinct targets; a source never sends to itself and sends its 6 requests to distinct targets. `lengths`: some request has exactly 128 tokens.
All inputs are finite; a program needn't handle non-finite values.
Results may differ from a plain program's by a relative error of at most 0.0062.
Values may be sent and summed in bfloat16 or wider, within the bound.
A program may use at most 128 MiB of HBM per device.

v0:
```python
import math

import jax
import jax.numpy as jnp
from jax import lax
from jax.sharding import PartitionSpec as P

ROPE_BASE = 1000000.0
HIGHEST = lax.Precision.HIGHEST


def sylvester(order):
    indices = jnp.arange(order, dtype=jnp.int32)
    common = jnp.bitwise_and(indices[:, None], indices[None, :])
    parity = jnp.zeros((order, order), dtype=jnp.int32)
    for level in range(order.bit_length() - 1):
        parity = parity + common // 2**level % 2
    return (1 - 2 * (parity % 2)).astype(jnp.bfloat16)


def rotary(vectors, places):
    width = vectors.shape[-1]
    half = width // 2
    exponents = jnp.arange(half, dtype=jnp.float32) * (2.0 / width)
    frequency = jnp.power(jnp.float32(ROPE_BASE), -exponents)
    angles = places.astype(jnp.float32)[..., None] * frequency
    cosine = jnp.cos(angles)
    sine = jnp.sin(angles)
    first = vectors[..., :half]
    second = vectors[..., half:]
    return jnp.concatenate(
        [first * cosine - second * sine, second * cosine + first * sine], axis=-1
    )


def unchanged(values):
    return values


def decode_step(
    query_cache, query_fresh, cache_keys, cache_values, valid, fresh_keys, fresh_values, finish
):
    factor = 1.0 / math.sqrt(query_cache.shape[-1])
    cached = jnp.einsum("rkgd,rkpd->rkgp", query_cache, cache_keys, precision=HIGHEST) * factor
    cached = jnp.where(valid[:, None, None, :], cached, -jnp.inf)
    recent = jnp.einsum("rkgd,rkud->rkgu", query_fresh, fresh_keys, precision=HIGHEST) * factor
    top = jnp.maximum(jnp.max(cached, axis=-1), jnp.max(recent, axis=-1))[..., None]
    cached_weight = jnp.exp(cached - top)
    recent_weight = jnp.exp(recent - top)
    total = jnp.sum(cached_weight, axis=-1) + jnp.sum(recent_weight, axis=-1)
    mixed = finish(jnp.einsum("rkgp,rkpd->rkgd", cached_weight, cache_values, precision=HIGHEST))
    mixed = mixed + jnp.einsum("rkgu,rkud->rkgd", recent_weight, fresh_values, precision=HIGHEST)
    return mixed / total[..., None]


def on_device(source_cache, block_table, lengths, target_map, queries, fresh_cache, positions):
    instances = lax.axis_size("inst")
    ranks = lax.axis_size("tp")
    here = lax.axis_index("inst")
    rank_here = lax.axis_index("tp")
    pages = source_cache[0][block_table[0]]
    requests, heads, pair, half, width = pages.shape
    local_heads = heads // ranks
    hadamard = sylvester(width)
    hadamard_wide = hadamard.astype(jnp.float32)
    inv_root = 1.0 / math.sqrt(width)
    rotated = (
        jnp.dot(pages.reshape(-1, width), hadamard, preferred_element_type=jnp.float32) * inv_root
    )
    rotated = rotated.reshape(pages.shape)
    own_lengths = lax.dynamic_index_in_dim(lengths, here, 0, keepdims=False)
    tokens = rank_here * half + jnp.arange(half, dtype=jnp.int32)
    valid = tokens[None, :] < own_lengths[:, None]
    rotated = jnp.where(valid[:, None, None, :, None], rotated, 0.0)
    local_max = jnp.max(jnp.abs(rotated), axis=(3, 4))
    block_max = lax.pmax(local_max, "tp")
    block_scale = (block_max + 1e-06).astype(jnp.bfloat16)
    quantized = (rotated / block_scale.astype(jnp.float32)[..., None, None]).astype(jnp.bfloat16)
    own_map = lax.dynamic_index_in_dim(target_map, here, 0, keepdims=False)
    matches = own_map[None, :] == jnp.arange(instances, dtype=jnp.int32)[:, None]
    chosen = jnp.sum(jnp.where(matches, jnp.arange(requests, dtype=jnp.int32)[None, :], 0), axis=1)
    present = jnp.any(matches, axis=1)
    outgoing = jnp.where(present[:, None, None, None, None], quantized[chosen], 0)
    outgoing_scale = jnp.where(present[:, None, None], block_scale[chosen], 0)
    hits = target_map == here
    source_of = jnp.sum(jnp.where(hits, jnp.arange(instances, dtype=jnp.int32)[:, None], 0), axis=0)
    slot_ids = jnp.arange(requests, dtype=jnp.int32)
    valid_len = lengths[source_of, slot_ids]
    page_size = ranks * half
    flat_pages = outgoing.reshape(instances * ranks, local_heads, pair, half, width)
    flat_scale = outgoing_scale.reshape(instances * ranks, local_heads, pair)
    arrived, arrived_scale = (
        lax.all_to_all(flat_pages, ("inst", "tp"), split_axis=0, concat_axis=0, tiled=True),
        lax.all_to_all(flat_scale, ("inst", "tp"), split_axis=0, concat_axis=0, tiled=True),
    )
    gathered = arrived.reshape(instances, ranks, local_heads, pair, half, width)[source_of]
    migrated = gathered.transpose(0, 2, 3, 1, 4, 5).reshape(
        requests, local_heads, pair, page_size, width
    )
    scales = arrived_scale.reshape(instances, ranks, local_heads, pair)[source_of, 0]
    restored = migrated.astype(jnp.float32) * scales.astype(jnp.float32)[..., None, None]
    steps = queries.shape[0]
    local_queries = queries.shape[3]
    group = local_queries // local_heads
    page_tokens = jnp.arange(page_size, dtype=jnp.int32)
    valid_page = page_tokens[None, :] < valid_len[:, None]
    places = positions[0][None, :] + jnp.arange(steps, dtype=jnp.int32)[:, None]
    fresh_rows = fresh_cache[:, 0]
    fresh_keys = rotary(fresh_rows[:, :, :, 0].astype(jnp.float32), places[:, :, None])
    fresh_keys = jnp.transpose(fresh_keys, (1, 2, 0, 3))
    fresh_values = jnp.transpose(fresh_rows[:, :, :, 1].astype(jnp.float32), (1, 2, 0, 3))
    restored_back = (
        jnp.einsum("rkepd,dc->rkepc", restored, hadamard_wide, precision=HIGHEST) * inv_root
    )
    cache_keys = restored_back[:, :, 0]
    cache_values = restored_back[:, :, 1]
    outputs = []
    for step in range(steps):
        query_rot = rotary(queries[step, 0].astype(jnp.float32), places[step][:, None])
        query_rot = query_rot.reshape(requests, local_heads, group, width)
        mixed = decode_step(
            unchanged(query_rot),
            query_rot,
            cache_keys,
            cache_values,
            valid_page,
            fresh_keys[:, :, : step + 1],
            fresh_values[:, :, : step + 1],
            unchanged,
        )
        outputs.append(mixed.reshape(requests, local_queries, width))
    attended = jnp.stack(outputs).astype(jnp.bfloat16)[:, None]
    return (scales[None], attended)


def solution(mesh):
    return jax.shard_map(
        on_device,
        mesh=mesh,
        in_specs=(
            P(("groups", "inst"), None, None, None, "tp", None),
            P(("groups", "inst"), None),
            P("groups", None),
            P("groups", None),
            P(None, ("groups", "inst"), None, "tp", None),
            P(None, ("groups", "inst"), None, "tp", None, None),
            P(("groups", "inst"), None),
        ),
        out_specs=(
            P(("groups", "inst"), None, "tp", None),
            P(None, ("groups", "inst"), None, "tp", None),
        ),
        check_vma=False,
    )
```

profile of v0, /device:TPU:15, one launch (start us, length us, event | category | flops | bytes accessed | tf_op | source)
XLA Modules:
  0.0 70.2 jit_solution(18111037596495484281)
XLA Ops:
  0.6 0.8 %dynamic-slice_bitcast_fusion = (s32[6]{0:T(128)S(1)}, s32[6]{0:T(128)S(1)}) fusion(s32[8,6]{1,0:T(8,128)} %param.9, s32[]{:T(128)S(6)} %select_n.167, s32[8,6]{1,0:T(8,128)} %param.10), kind=kLoop, calls=%fused_computation.253 | loop fusion | bytes 100 | tf_op jit(solution)/shard_map/lt | solution.py:73
  1.9 0.7 fusion.90
  2.5 0.7 gather_fusion
  3.2 1.2 %abs_reduce_fusion = (f32[3072]{0:T(1024)S(1)}, f32[3072,128]{1,0:T(8,128)S(1)}) fusion(pred[3072]{0:T(1024)(128)(4,1)S(1)} %broadcast_in_dim.164, bf16[3072,128]{1,0:T(8,128)(2,1)S(1)} %bitcast.170), kind=kOutput, calls=%fused_computation.10 | convolution fusion | flops 104788992 | bytes 2374656 | tf_op jit(solution)/shard_map/dot_general | solution.py:68
  4.7 2.8 %pmax.7 = f32[6,4,2]{0,1,2:T(4,128)S(1)} all-reduce(f32[6,4,2]{0,1,2:T(4,128)S(1)} %copy.57), channel_id=1, replica_groups=mesh['groups'=2,'inst'=8,'tp'=2] {'tp'}, use_global_device_ids=true, to_apply=%region_3.4 | all-reduce | flops 48 | bytes 384 | tf_op jit(solution)/shard_map/pmax | solution.py:76
  7.6 0.6 gather_fusion.1
  8.6 0.6 copy.60
  9.2 6.2 %all-to-all-start = ((bf16[16,2,2]{1,2,0:T(2,128)(2,1)}), bf16[16,2,2]{1,2,0:T(2,128)(2,1)S(1)}, u32[]{:S(2)}, u32[]{:S(2)}) async-start(bf16[16,2,2]{1,2,0:T(2,128)(2,1)} %copy.60), calls=%async_computation | async-start | bytes 16384 | tf_op jit(solution)/shard_map/all_to_all | solution.py:94
  15.6 0.3 divide_convert_fusion
  15.9 0.7 %gather_fusion.4 = bf16[8,4,2,64,128]{4,3,2,1,0:T(8,128)(2,1)S(1)} fusion(bf16[6,4,2,64,128]{4,3,2,1,0:T(8,128)(2,1)S(1)} %divide_convert_fusion, s32[1024]{0:T(1024)S(1)} %pad_clamp_fusion.1), kind=kCustom, calls=%fused_computation.4 | custom fusion | bytes 2097184 | tf_op jit(solution)/shard_map/gather | solution.py:83
  16.7 1.1 %broadcast_select_fusion = bf16[16,2,2,64,128]{4,3,2,1,0:T(8,128)(2,1)} fusion(bf16[16,2,2,64,128]{4,3,2,1,0:T(8,128)(2,1)S(1)} %bitcast.155, pred[16]{0:T(512)(128)(4,1)S(1)} %broadcast_in_dim.103), kind=kLoop, calls=%fused_computation.47 | loop fusion | flops 524288 | bytes 2097168 | tf_op jit(solution)/shard_map/jit(_where)/select_n | solution.py:83
  19.5 6.0 %all-to-all-start.1 = ((bf16[16,2,2,64,128]{4,3,2,1,0:T(8,128)(2,1)}), bf16[16,2,2,64,128]{4,3,2,1,0:T(8,128)(2,1)S(1)}, u32[]{:S(2)}, u32[]{:S(2)}) async-start(bf16[16,2,2,64,128]{4,3,2,1,0:T(8,128)(2,1)} %broadcast_select_fusion), calls=%async_computation.1 | async-start | bytes 2097152 | tf_op jit(solution)/shard_map/all_to_all | solution.py:93
  25.6 0.6 gather_fusion.3
  26.4 0.3 fusion.86
  26.7 0.3 fusion.121
  27.0 0.3 fusion.123
  27.3 0.3 fusion.125
  27.6 0.3 fusion.127
  27.9 0.3 fusion.129
  28.2 0.2 copy.62
  28.4 0.6 gather_fusion.2
  29.0 0.7 copy.63
  29.6 20.8 %all-to-all-done.1 = bf16[16,2,2,64,128]{4,3,2,1,0:T(8,128)(2,1)S(1)} async-done(((bf16[16,2,2,64,128]{4,3,2,1,0:T(8,128)(2,1)}), bf16[16,2,2,64,128]{4,3,2,1,0:T(8,128)(2,1)S(1)}, u32[]{:S(2)}, u32[]{:S(2)}) %all-to-all-start.1) | async-done | bytes 1048608 | tf_op jit(solution)/shard_map/all_to_all | solution.py:93
  50.4 0.7 gather_fusion.5
  51.6 1.1 %convolution_multiply_fusion.1 = f32[6,2,2,128,128]{4,3,2,1,0:T(8,128)S(1)} fusion(f32[6,2,2,128,128]{4,3,2,1,0:T(8,128)S(1)} %bitcast_multiply_fusion), kind=kOutput, calls=%fused_computation.11 | convolution fusion | flops 606928896 | bytes 3145728 | tf_op jit(solution)/shard_map/rkepd,dc->rkepc/dot_general | solution.py:113
  52.7 1.4 %fusion.119 = (f32[6,2,16]{2,1,0:T(2,128)S(1)}, f32[6,2,16,128]{3,2,1,0:T(8,128)S(1)}) fusion(f32[6,2,16,128]{3,2,1,0:T(8,128)S(1)} %bitcast.161, f32[6,2,2,128,128]{4,3,2,1,0:T(8,128)S(1)} %convolution_multiply_fusion.1, pred[6,128]{1,0:T(8,128)(4,1)S(1)} %iota_compare_fusion), kind=kOutput, calls=%fused_computation.283 | convolution fusion | flops 37822272 | bytes 984832 | tf_op jit(solution)/shard_map/rkgd,rkpd->rkgp/dot_general | solution.py:44
  54.1 1.4 %fusion.120 = (f32[6,2,16]{2,1,0:T(2,128)S(1)}, f32[6,2,16,128]{3,2,1,0:T(8,128)S(1)}) fusion(f32[6,2,16,128]{3,2,1,0:T(8,128)S(1)} %bitcast.163, f32[6,2,2,128,128]{4,3,2,1,0:T(8,128)S(1)} %convolution_multiply_fusion.1, pred[6,128]{1,0:T(8,128)(4,1)S(1)} %iota_compare_fusion), kind=kOutput, calls=%fused_computation.284 | convolution fusion | flops 37822272 | bytes 984832 | tf_op jit(solution)/shard_map/rkgd,rkpd->rkgp/dot_general | solution.py:44
  55.6 0.8 %fusion.22 = f32[6,2,16,128]{3,2,1,0:T(8,128)S(1)} fusion(f32[6,2,2,128,128]{4,3,2,1,0:T(8,128)S(1)} %convolution_multiply_fusion.1, f32[6,2,16,128]{3,2,1,0:T(8,128)S(1)} %get-tuple-element.66, f32[6,2,16]{2,1,0:T(2,128)S(1)} %max.43), kind=kOutput, calls=%fused_computation.54 | convolution fusion | flops 37773312 | bytes 989184 | tf_op jit(solution)/shard_map/rkgp,rkpd->rkgd/dot_general | solution.py:51
  56.4 0.2 fusion.24
  56.6 1.4 %fusion.122 = (f32[6,2,16]{2,1,0:T(2,128)S(1)}, f32[6,2,16,128]{3,2,1,0:T(8,128)S(1)}) fusion(f32[6,2,16,128]{3,2,1,0:T(8,128)S(1)} %bitcast.167, f32[6,2,2,128,128]{4,3,2,1,0:T(8,128)S(1)} %convolution_multiply_fusion.1, pred[6,128]{1,0:T(8,128)(4,1)S(1)} %iota_compare_fusion), kind=kOutput, calls=%fused_computation.286 | convolution fusion | flops 37822272 | bytes 984832 | tf_op jit(solution)/shard_map/rkgd,rkpd->rkgp/dot_general | solution.py:44
  58.0 0.8 %fusion.21 = f32[6,2,16,128]{3,2,1,0:T(8,128)S(1)} fusion(f32[6,2,2,128,128]{4,3,2,1,0:T(8,128)S(1)} %convolution_multiply_fusion.1, f32[6,2,16,128]{3,2,1,0:T(8,128)S(1)} %get-tuple-element.70, f32[6,2,16]{2,1,0:T(2,128)S(1)} %max.44), kind=kOutput, calls=%fused_computation.53 | convolution fusion | flops 37773312 | bytes 989184 | tf_op jit(solution)/shard_map/rkgp,rkpd->rkgd/dot_general | solution.py:51
  58.9 0.2 fusion.25
  59.1 1.4 %fusion.124 = (f32[6,2,16]{2,1,0:T(2,128)S(1)}, f32[6,2,16,128]{3,2,1,0:T(8,128)S(1)}) fusion(f32[6,2,16,128]{3,2,1,0:T(8,128)S(1)} %bitcast.159, f32[6,2,2,128,128]{4,3,2,1,0:T(8,128)S(1)} %convolution_multiply_fusion.1, pred[6,128]{1,0:T(8,128)(4,1)S(1)} %iota_compare_fusion), kind=kOutput, calls=%fused_computation.288 | convolution fusion | flops 37822272 | bytes 984832 | tf_op jit(solution)/shard_map/rkgd,rkpd->rkgp/dot_general | solution.py:44
  60.5 0.8 %fusion.20 = f32[6,2,16,128]{3,2,1,0:T(8,128)S(1)} fusion(f32[6,2,2,128,128]{4,3,2,1,0:T(8,128)S(1)} %convolution_multiply_fusion.1, f32[6,2,16,128]{3,2,1,0:T(8,128)S(1)} %get-tuple-element.74, f32[6,2,16]{2,1,0:T(2,128)S(1)} %max.45), kind=kOutput, calls=%fused_computation.52 | convolution fusion | flops 37773312 | bytes 989184 | tf_op jit(solution)/shard_map/rkgp,rkpd->rkgd/dot_general | solution.py:51
  61.3 0.2 fusion.26
  61.5 1.4 %fusion.126 = (f32[6,2,16]{2,1,0:T(2,128)S(1)}, f32[6,2,16,128]{3,2,1,0:T(8,128)S(1)}) fusion(f32[6,2,16,128]{3,2,1,0:T(8,128)S(1)} %bitcast.165, f32[6,2,2,128,128]{4,3,2,1,0:T(8,128)S(1)} %convolution_multiply_fusion.1, pred[6,128]{1,0:T(8,128)(4,1)S(1)} %iota_compare_fusion), kind=kOutput, calls=%fused_computation.290 | convolution fusion | flops 37822272 | bytes 984832 | tf_op jit(solution)/shard_map/rkgd,rkpd->rkgp/dot_general | solution.py:44
  63.0 0.8 %fusion.19 = f32[6,2,16,128]{3,2,1,0:T(8,128)S(1)} fusion(f32[6,2,2,128,128]{4,3,2,1,0:T(8,128)S(1)} %convolution_multiply_fusion.1, f32[6,2,16,128]{3,2,1,0:T(8,128)S(1)} %get-tuple-element.78, f32[6,2,16]{2,1,0:T(2,128)S(1)} %max.46), kind=kOutput, calls=%fused_computation.51 | convolution fusion | flops 37773312 | bytes 989184 | tf_op jit(solution)/shard_map/rkgp,rkpd->rkgd/dot_general | solution.py:51
  63.8 0.2 fusion.27
  64.0 1.4 %fusion.128 = (f32[6,2,16]{2,1,0:T(2,128)S(1)}, f32[6,2,16,128]{3,2,1,0:T(8,128)S(1)}) fusion(f32[6,2,16,128]{3,2,1,0:T(8,128)S(1)} %bitcast.169, f32[6,2,2,128,128]{4,3,2,1,0:T(8,128)S(1)} %convolution_multiply_fusion.1, pred[6,128]{1,0:T(8,128)(4,1)S(1)} %iota_compare_fusion), kind=kOutput, calls=%fused_computation.292 | convolution fusion | flops 37822272 | bytes 984832 | tf_op jit(solution)/shard_map/rkgd,rkpd->rkgp/dot_general | solution.py:44
  65.4 0.8 %fusion.18 = f32[6,2,16,128]{3,2,1,0:T(8,128)S(1)} fusion(f32[6,2,2,128,128]{4,3,2,1,0:T(8,128)S(1)} %convolution_multiply_fusion.1, f32[6,2,16,128]{3,2,1,0:T(8,128)S(1)} %get-tuple-element.82, f32[6,2,16]{2,1,0:T(2,128)S(1)} %max.47), kind=kOutput, calls=%fused_computation.50 | convolution fusion | flops 37773312 | bytes 989184 | tf_op jit(solution)/shard_map/rkgp,rkpd->rkgd/dot_general | solution.py:51
  66.3 0.2 fusion.28
  66.7 0.8 %fusion.12 = bf16[6,2,16,128]{3,2,1,0:T(8,128)(2,1)S(1)} fusion(f32[6,2,2,128,128]{4,3,2,1,0:T(8,128)S(1)} %convolution_multiply_fusion.1, f32[6,2,16,128]{3,2,1,0:T(8,128)S(1)} %get-tuple-element.64, f32[6,2,16]{2,1,0:T(2,128)S(1)} %get-tuple-element.2, f32[6,2,128]{2,1,0:T(2,128)S(1)} %bitcast.182, f32[6,2,16]{2,1,0:T(2,128)S(1)} %get-tuple-element.3, ...), kind=kOutput, calls=%fused_computation.36 | convolution fusion | flops 37871616 | bytes 958464 | tf_op jit(solution)/shard_map/rkgp,rkpd->rkgd/dot_general | solution.py:51
  67.8 0.3 fusion.13
  68.1 0.3 fusion.14
  68.5 0.3 fusion.15
  68.8 0.3 fusion.16
  69.2 0.3 fusion.17
  69.5 0.7 %copy-done.4 = bf16[6,1,6,32,128]{4,3,2,1,0:T(8,128)(2,1)} copy-done((bf16[6,1,6,32,128]{4,3,2,1,0:T(8,128)(2,1)}, bf16[6,1,6,32,128]{4,3,2,1,0:T(8,128)(2,1)S(1)}, u32[]{:S(2)}) %copy-start.4) | copy-done | bytes 294936
  (87 shorter events, 4.1 us)
Async XLA Ops:
  0.6 1.9 %copy-start = (bf16[1,6,4,2,64,128]{5,4,3,2,1,0:T(8,128)(2,1)S(1)}, bf16[1,6,4,2,64,128]{5,4,3,2,1,0:T(8,128)(2,1)}, u32[]{:S(2)}) copy-start(bf16[1,6,4,2,64,128]{5,4,3,2,1,0:T(8,128)(2,1)} %param.7) | copy-start | bytes 2359300
  3.2 12.2 %copy-start.5 = (s32[8,6]{1,0:T(8,128)S(1)}, s32[8,6]{1,0:T(8,128)}, u32[]{:S(2)}) copy-start(s32[8,6]{1,0:T(8,128)} %param.10) | copy-start | bytes 580
  9.2 10.3 %all-to-all-start = ((bf16[16,2,2]{1,2,0:T(2,128)(2,1)}), bf16[16,2,2]{1,2,0:T(2,128)(2,1)S(1)}, u32[]{:S(2)}, u32[]{:S(2)}) async-start(bf16[16,2,2]{1,2,0:T(2,128)(2,1)} %copy.60), calls=%async_computation | async-start | bytes 16384 | tf_op jit(solution)/shard_map/all_to_all | solution.py:94
  16.7 1.2 %copy-start.2 = (bf16[6,1,6,32,128]{4,3,2,1,0:T(8,128)(2,1)S(1)}, bf16[6,1,6,32,128]{4,3,2,1,0:T(8,128)(2,1)}, u32[]{:S(2)}) copy-start(bf16[6,1,6,32,128]{4,3,2,1,0:T(8,128)(2,1)} %param.11) | copy-start | bytes 884740
  16.7 1.2 %copy-start.6 = (s32[1,6]{1,0:T(1,128)S(1)}, s32[1,6]{1,0:T(1,128)}, u32[]{:S(2)}) copy-start(s32[1,6]{1,0:T(1,128)} %param.13) | copy-start | bytes 76
  16.7 1.2 %copy-start.3 = (bf16[6,1,6,2,2,128]{5,4,3,2,1,0:T(2,128)(2,1)S(1)}, bf16[6,1,6,2,2,128]{5,4,3,2,1,0:T(2,128)(2,1)}, u32[]{:S(2)}) copy-start(bf16[6,1,6,2,2,128]{5,4,3,2,1,0:T(2,128)(2,1)} %param.12) | copy-start | bytes 110596
  19.2 6.3 %copy-start.1 = (s32[8,6]{1,0:T(8,128)S(1)}, s32[8,6]{1,0:T(8,128)}, u32[]{:S(2)}) copy-start(s32[8,6]{1,0:T(8,128)} %param.9) | copy-start | bytes 580
  19.5 30.9 %all-to-all-start.1 = ((bf16[16,2,2,64,128]{4,3,2,1,0:T(8,128)(2,1)}), bf16[16,2,2,64,128]{4,3,2,1,0:T(8,128)(2,1)S(1)}, u32[]{:S(2)}, u32[]{:S(2)}) async-start(bf16[16,2,2,64,128]{4,3,2,1,0:T(8,128)(2,1)} %broadcast_select_fusion), calls=%async_computation.1 | async-start | bytes 2097152 | tf_op jit(solution)/shard_map/all_to_all | solution.py:93
  69.5 0.7 %copy-start.4 = (bf16[6,1,6,32,128]{4,3,2,1,0:T(8,128)(2,1)}, bf16[6,1,6,32,128]{4,3,2,1,0:T(8,128)(2,1)S(1)}, u32[]{:S(2)}) copy-start(bf16[6,1,6,32,128]{4,3,2,1,0:T(8,128)(2,1)S(1)} %constant_dynamic-update-slice_fusion) | copy-start | bytes 884740
where the time goes:
time: 70.5 us; the launch traced here: 70.2 us
  waiting for transfers between devices  20.8 us (30%)
  matrix products  19.1 us (27%)
  starting transfers between devices  12.3 us (17%)
  local copies, waits for them, and re-layouts  8.04 us (11%)
  other arithmetic  6.12 us (9%)
  blocking collectives  2.79 us (4%)
  between operations  1.17 us (2%)
    all_to_all x1, waiting for transfers between devices, on_device(): lax.all_to_all(flat_pages, ('inst', 'tp'), split_axis=0, concat_axis=0, t...  20.8 us
    dot_general x6, matrix products, decode_step(): jnp.einsum('rkgd,rkpd->rkgp', query_cache, cache_keys, precision=HIGHEST)  8.49 us
    all_to_all x1, starting transfers between devices, on_device(): lax.all_to_all(flat_scale, ('inst', 'tp'), split_axis=0, concat_axis=0, t...  6.22 us
    all_to_all x1, starting transfers between devices, on_device(): lax.all_to_all(flat_pages, ('inst', 'tp'), split_axis=0, concat_axis=0, t...  6.03 us
    dot_general x6, matrix products, decode_step(): jnp.einsum('rkgp,rkpd->rkgd', cached_weight, cache_values, precision=HIGH...  5.01 us
    pmax x1, blocking collectives, on_device(): block_max = lax.pmax(local_max, 'tp')  2.79 us
    dot_general x6, matrix products, decode_step(): jnp.einsum('rkgd,rkud->rkgu', query_fresh, fresh_keys, precision=HIGHEST)  1.77 us
    dot_general x5, matrix products, decode_step(): jnp.einsum('rkgu,rkud->rkgd', recent_weight, fresh_values, precision=HIGH...  1.53 us
  transfers between devices with their start and end apart: 2, of which 1 were waited for; matrix products, arithmetic and copies ran while one was open for 11% of the time, Pallas kernels for 0%

commit v1 on v0

v1 whole, which is shorter than its diff:
```python
import functools
import math

import jax
import jax.numpy as jnp
from jax import lax
from jax.experimental import pallas as pl
from jax.experimental.pallas import tpu as pltpu
from jax.sharding import PartitionSpec as P

ROPE_BASE = 1000000.0
HIGHEST = lax.Precision.HIGHEST
MESH = pl.DeviceIdType.MESH
F32 = jnp.float32
BF16 = jnp.bfloat16


def sylvester(order):
    rows = lax.broadcasted_iota(jnp.int32, (order, order), 0)
    columns = lax.broadcasted_iota(jnp.int32, (order, order), 1)
    common = jnp.bitwise_and(rows, columns)
    parity = jnp.zeros((order, order), dtype=jnp.int32)
    for level in range(order.bit_length() - 1):
        parity = parity + jnp.bitwise_and(lax.shift_right_logical(common, level), 1)
    return (1 - 2 * jnp.bitwise_and(parity, 1)).astype(F32).astype(BF16)


def split(values):
    high = values.astype(BF16)
    low = (values - high.astype(F32)).astype(BF16)
    return high, low


def dot(a, b):
    return jnp.dot(a, b, preferred_element_type=F32)


def dot_t(a, b, precision=None):
    return lax.dot_general(
        a, b, (((1,), (1,)), ((), ())), precision=precision, preferred_element_type=F32
    )


def kernel(
    n,
    table_ref,
    length_ref,
    map_ref,
    cache_ref,
    query_ref,
    fresh_ref,
    turn_ref,
    out_ref,
    scale_ref,
    had,
    other,
    quant,
    scale,
    ask,
    asked,
    turns,
    turned,
    reply,
    replied,
    swap_sem,
    ask_send,
    ask_recv,
    turn_send,
    turn_recv,
    reply_send,
    reply_recv,
):
    group = lax.axis_index("groups")
    me = lax.axis_index("inst")
    rank = lax.axis_index("tp")
    steps, _, requests, query_heads, width = query_ref.shape
    heads = cache_ref.shape[1] // 2
    half = cache_ref.shape[3]
    share = query_heads // heads
    rows = steps * share
    asks = heads * rows
    factor = 1.0 / math.sqrt(width)

    def after(d):
        return lax.rem(me + d, n)

    def before(d):
        return lax.rem(me + n - d, n)

    barrier = pltpu.get_barrier_semaphore()

    pl.semaphore_signal(barrier, inc=1, device_id=(group, me, 1 - rank), device_id_type=MESH)

    @pl.loop(1, n)
    def _(d):
        pl.semaphore_signal(barrier, inc=1, device_id=(group, after(d), rank), device_id_type=MESH)

    had[...] = sylvester(width)
    pl.semaphore_wait(barrier, n)

    swap = pltpu.make_async_remote_copy(
        src_ref=cache_ref.at[:, pl.ds((1 - rank) * heads, heads)],
        dst_ref=other,
        send_sem=swap_sem.at[0],
        recv_sem=swap_sem.at[1],
        device_id=(group, me, 1 - rank),
        device_id_type=MESH,
    )
    swap.start()

    def ask_copy(d, slot, target):
        return pltpu.make_async_remote_copy(
            src_ref=ask.at[after(d)],
            dst_ref=asked.at[slot],
            send_sem=ask_send.at[d],
            recv_sem=ask_recv.at[d],
            device_id=(group, target, rank),
            device_id_type=MESH,
        )

    def turn_copy(d, slot, target):
        return pltpu.make_async_remote_copy(
            src_ref=turns.at[after(d)],
            dst_ref=turned.at[slot],
            send_sem=turn_send.at[d],
            recv_sem=turn_recv.at[d],
            device_id=(group, target, rank),
            device_id_type=MESH,
        )

    def reply_copy(d, slot, target):
        return pltpu.make_async_remote_copy(
            src_ref=reply.at[before(d)],
            dst_ref=replied.at[slot],
            send_sem=reply_send.at[d],
            recv_sem=reply_recv.at[d],
            device_id=(group, target, rank),
            device_id_type=MESH,
        )

    @pl.loop(1, n)
    def _(d):
        source = after(d)
        chosen = jnp.int32(0)
        for j in range(requests):
            chosen = jnp.maximum(chosen, jnp.where(map_ref[source, j] == me, j, 0))
        for g in range(heads):
            for u in range(steps):
                ask[source, pl.ds(g * rows + u * share, share), :] = query_ref[
                    u, 0, chosen, pl.ds(g * share, share), :
                ]
        ask[source, pl.ds(asks, 32), :] = fresh_ref[chosen]
        turns[source] = turn_ref[chosen]
        turn_copy(d, me, source).start()
        ask_copy(d, me, source).start()

    swap.wait_recv()

    token = lax.broadcasted_iota(jnp.int32, (2 * half, width), 0)
    token = jnp.where(token < half, token + rank * half, token - half + (1 - rank) * half)
    line = lax.broadcasted_iota(jnp.int32, (16, width), 0)

    @pl.loop(0, requests)
    def _(j):
        page = table_ref[0, j]
        keep = token < length_ref[me, j]
        signs = had[...]
        packed = jnp.zeros((16, width), F32)
        for g in range(heads):
            for e in range(2):
                values = jnp.concatenate(
                    [cache_ref[page, rank * heads + g, e], other[page, g, e]], axis=0
                )
                rotated = jnp.where(keep, dot(values, signs) * factor, 0.0)
                top = jnp.max(jnp.max(jnp.abs(rotated), axis=0, keepdims=True), axis=1, keepdims=True)
                block = (jnp.broadcast_to(top, (16, width)) + 1e-06).astype(BF16).astype(F32)
                packed = jnp.where(line == 2 * g + e, block, packed)
                quant[j, g, e] = (rotated / block[:1]).astype(BF16)
        scale[j] = packed

    lane = lax.broadcasted_iota(jnp.int32, (8, width), 1)
    row = lax.broadcasted_iota(jnp.int32, (rows, 8), 0)
    later = lax.broadcasted_iota(jnp.int32, (rows, 8), 1)
    open_ = later * share <= row
    column = lax.broadcasted_iota(jnp.int32, (rows, 2 * half), 1)
    column = jnp.where(column < half, column + rank * half, column - half + (1 - rank) * half)

    @pl.loop(1, n)
    def _(d):
        target = before(d)
        turn_copy(d, target, target).wait_recv()
        ask_copy(d, target, target).wait_recv()
        chosen = jnp.int32(0)
        for j in range(requests):
            chosen = jnp.maximum(chosen, jnp.where(map_ref[me, j] == target, j, 0))
        keep = column < length_ref[me, chosen]
        signs = had[...]
        packed = scale[chosen]
        turn = turned[target]
        flipped = pltpu.roll(turn, width // 2, 1)
        cosine = jnp.where(lane < width // 2, turn, flipped)
        sine = jnp.where(lane < width // 2, -flipped, turn)
        wide_cosine = jnp.concatenate(
            [jnp.broadcast_to(cosine[u : u + 1], (share, width)) for u in range(steps)], axis=0
        )
        wide_sine = jnp.concatenate(
            [jnp.broadcast_to(sine[u : u + 1], (share, width)) for u in range(steps)], axis=0
        )
        fresh = asked[target, pl.ds(asks, 32), :].astype(F32)
        for g in range(heads):
            query = asked[target, pl.ds(g * rows, rows), :].astype(F32)
            query = query * wide_cosine + pltpu.roll(query, width // 2, 1) * wide_sine
            key = fresh[16 * g : 16 * g + 8]
            key = key * cosine + pltpu.roll(key, width // 2, 1) * sine
            value = fresh[16 * g + 8 : 16 * g + 16]
            high, low = split(query)
            mixed_high, mixed_low = split(dot(high, signs) + dot(low, signs))
            keys = quant[chosen, g, 0]
            cached = dot_t(mixed_high, keys) + dot_t(mixed_low, keys)
            cached = cached * (packed[2 * g : 2 * g + 1] * (factor * factor))
            cached = jnp.where(keep, cached, -jnp.inf)
            recent = dot_t(query, key, HIGHEST) * factor
            recent = jnp.where(open_, recent, -jnp.inf)
            top = jnp.maximum(
                jnp.max(cached, axis=1, keepdims=True), jnp.max(recent, axis=1, keepdims=True)
            )
            cached = jnp.exp(cached - top)
            recent = jnp.exp(recent - top)
            total = jnp.sum(cached, axis=1, keepdims=True) + jnp.sum(recent, axis=1, keepdims=True)
            high, low = split(cached)
            values = quant[chosen, g, 1]
            mixed = (dot(high, values) + dot(low, values)) * (
                packed[2 * g + 1 : 2 * g + 2] * factor
            )
            high, low = split(mixed)
            mixed = dot(high, signs) + dot(low, signs)
            mixed = mixed + jnp.dot(recent, value, precision=HIGHEST, preferred_element_type=F32)
            reply[target, pl.ds(g * rows, rows), :] = (mixed / total).astype(BF16)
        reply[target, pl.ds(asks, 16), :] = packed.astype(BF16)
        reply_copy(d, me, target).start()

    @pl.loop(1, n)
    def _(d):
        source = after(d)
        reply_copy(d, source, source).wait_recv()

    @pl.loop(0, requests)
    def _(j):
        source = jnp.int32(0)
        for s in range(n):
            source = jnp.maximum(source, jnp.where(map_ref[s, j] == me, s, 0))
        for g in range(heads):
            for u in range(steps):
                out_ref[u, 0, j, pl.ds(g * share, share), :] = replied[
                    source, pl.ds(g * rows + u * share, share), :
                ]
        scale_ref[j] = replied[source, pl.ds(asks, 16), :]

    swap.wait_send()

    @pl.loop(1, n)
    def _(d):
        turn_copy(d, me, after(d)).wait_send()
        ask_copy(d, me, after(d)).wait_send()
        reply_copy(d, me, before(d)).wait_send()


def on_device(source_cache, block_table, lengths, target_map, queries, fresh_cache, positions):
    n = lax.axis_size("inst")
    _, requests, all_heads, pair, half, width = source_cache.shape
    steps = queries.shape[0]
    heads = fresh_cache.shape[3]
    asks = queries.shape[3] * steps
    exponents = jnp.arange(width // 2, dtype=F32) * (2.0 / width)
    frequency = jnp.power(F32(ROPE_BASE), -exponents)
    places = positions[0][:, None] + jnp.arange(8, dtype=jnp.int32)[None, :]
    angles = places.astype(F32)[..., None] * frequency
    turn = jnp.concatenate([jnp.cos(angles), jnp.sin(angles)], axis=-1)
    fresh = jnp.transpose(fresh_cache[:, 0], (1, 2, 3, 0, 4))
    fresh = jnp.pad(fresh, ((0, 0), (0, 0), (0, 0), (0, 8 - steps), (0, 0)))
    fresh = fresh.reshape(requests, heads * pair * 8, width)
    smem = pl.BlockSpec(memory_space=pltpu.SMEM)
    vmem = pl.BlockSpec(memory_space=pltpu.VMEM)
    dma = pltpu.SemaphoreType.DMA
    attended, scales = pl.pallas_call(
        functools.partial(kernel, n),
        out_shape=(
            jax.ShapeDtypeStruct(queries.shape, BF16),
            jax.ShapeDtypeStruct((requests, 16, width), BF16),
        ),
        in_specs=[smem] * 3 + [vmem] * 4,
        out_specs=(vmem, vmem),
        scratch_shapes=[
            pltpu.VMEM((width, width), BF16),
            pltpu.VMEM((requests, heads, pair, half, width), BF16),
            pltpu.VMEM((requests, heads, pair, 2 * half, width), BF16),
            pltpu.VMEM((requests, 16, width), F32),
            pltpu.VMEM((n, asks + 32, width), BF16),
            pltpu.VMEM((n, asks + 32, width), BF16),
            pltpu.VMEM((n, 8, width), F32),
            pltpu.VMEM((n, 8, width), F32),
            pltpu.VMEM((n, asks + 16, width), BF16),
            pltpu.VMEM((n, asks + 16, width), BF16),
            dma((2,)),
            dma((n,)),
            dma((n,)),
            dma((n,)),
            dma((n,)),
            dma((n,)),
            dma((n,)),
        ],
        compiler_params=pltpu.CompilerParams(
            collective_id=0, has_side_effects=True, vmem_limit_bytes=52 * 2**20
        ),
        cost_estimate=pl.CostEstimate(flops=10**9, bytes_accessed=4 * 10**6, transcendentals=10**5),
    )(block_table, lengths, target_map, source_cache[0], queries, fresh, turn)
    scales = scales[:, : heads * pair, 0].reshape(1, requests, heads, pair)
    return scales, attended


def solution(mesh):
    return jax.shard_map(
        on_device,
        mesh=mesh,
        in_specs=(
            P(("groups", "inst"), None, None, None, "tp", None),
            P(("groups", "inst"), None),
            P("groups", None),
            P("groups", None),
            P(None, ("groups", "inst"), None, "tp", None),
            P(None, ("groups", "inst"), None, "tp", None, None),
            P(("groups", "inst"), None),
        ),
        out_specs=(
            P(("groups", "inst"), None, "tp", None),
            P(None, ("groups", "inst"), None, "tp", None),
        ),
        check_vma=False,
    )
```

time: 70.5 us -> 40.4 us (0.57)
  the two profiles are of different devices: /device:TPU:15 before, /device:TPU:0 now
where the time goes in v1:
time: 40.4 us; the launch traced here: 40.1 us
  Pallas kernels  34.4 us (85%)
  local copies, waits for them, and re-layouts  3.99 us (10%)
  other arithmetic  1.02 us (3%)
  between operations  0.71 us (2%)
    pallas_call x1, Pallas kernels, on_device(): pl.pallas_call(functools.partial(kernel, n), out_shape=(jax.ShapeDtypeStr...  34.4 us
    unnamed x12, local copies, waits for them, and re-layouts  3.29 us

profile of v1, /device:TPU:0, one launch (start us, length us, event | category | flops | bytes accessed | tf_op | source)
XLA Modules:
  0.0 40.1 jit_solution(3455429170974628163)
XLA Ops:
  0.6 0.0 copy-start.1
  0.7 0.8 %add_convert_fusion = f32[6,8]{1,0:T(8,128)S(1)} fusion(s32[6]{0:T(128)} %bitcast.11), kind=kLoop, calls=%fused_computation.3 | loop fusion | flops 96 | bytes 216 | tf_op jit(solution)/shard_map/convert_element_type | solution.py:277
  1.4 0.2 multiply_cosine_fusion
  1.6 0.1 pad_maximum_fusion.turn_ref
  1.7 0.8 %copy.11 = bf16[6,2,2,6,128]{4,3,2,1,0:T(8,128)(2,1)S(1)} copy(bf16[6,2,2,6,128]{4,2,1,0,3:T(2,128)(2,1)} %bitcast.9) | data formatting | bytes 73728
  2.5 0.0 copy-start.2
  2.5 0.0 copy-start.3
  2.5 0.0 copy-start.4
  2.5 0.0 copy-done.1
  2.5 0.6 %copy-done.2 = s32[8,6]{1,0:T(8,128)S(1)} copy-done((s32[8,6]{1,0:T(8,128)S(1)}, s32[8,6]{1,0:T(8,128)}, u32[]{:S(2)}) %copy-start.2) | copy-done | bytes 216
  3.2 0.0 copy-done.3
  3.2 0.0 copy-done.4
  3.2 0.0 copy-start
  3.2 1.1 %copy-done = bf16[1,6,4,2,64,128]{5,4,3,2,1,0:T(8,128)(2,1)S(1)} copy-done((bf16[1,6,4,2,64,128]{5,4,3,2,1,0:T(8,128)(2,1)S(1)}, bf16[1,6,4,2,64,128]{5,4,3,2,1,0:T(8,128)(2,1)}, u32[]{:S(2)}) %copy-start) | copy-done | bytes 786456
  4.3 34.4 %shard_map.86 = (bf16[6,1,6,32,128]{4,3,2,1,0:T(8,128)(2,1)S(1)}, bf16[6,16,128]{2,1,0:T(8,128)(2,1)S(1)}) custom-call(s32[1,6]{1,0:T(1,128)S(1)} %copy-done.4, s32[8,6]{1,0:T(8,128)S(1)} %copy-done.2, s32[8,6]{1,0:T(8,128)S(1)} %copy-done.3, bf16[6,4,2,64,128]{4,3,2,1,0:T(8,128)(2,1)S(1)} %bitcast.8, bf16[6,1,6,32,128]{4,3,2,1,0:T(8,128)(2,1)S(1)} %copy-done.1, ...), custom_call_target="tpu_custom_call" | custom-call | flops 1000000000 | bytes 4000000 | tf_op jit(solution)/shard_map/pallas_call | solution.py:285
  38.7 0.7 %copy.10 = bf16[6,4,1]{0,1,2:T(4,128)(2,1)} copy(bf16[6,4,1]{2,1,0:T(4,128)(2,1)S(1)} %slice.3) | data formatting | bytes 96 | tf_op jit(solution)/shard_map/slice | solution.py:317
  39.4 0.7 %copy.13 = bf16[6,1,6,32,128]{4,3,2,1,0:T(8,128)(2,1)} copy(bf16[6,1,6,32,128]{4,3,2,1,0:T(8,128)(2,1)S(1)} %get-tuple-element.11) | data formatting | bytes 589824
  (3 shorter events, 0.0 us)
Async XLA Ops:
  0.6 1.9 %copy-start.1 = (bf16[6,1,6,32,128]{4,3,2,1,0:T(8,128)(2,1)S(1)}, bf16[6,1,6,32,128]{4,3,2,1,0:T(8,128)(2,1)}, u32[]{:S(2)}) copy-start(bf16[6,1,6,32,128]{4,3,2,1,0:T(8,128)(2,1)} %query_ref.1) | copy-start | bytes 884740
  2.5 0.7 %copy-start.2 = (s32[8,6]{1,0:T(8,128)S(1)}, s32[8,6]{1,0:T(8,128)}, u32[]{:S(2)}) copy-start(s32[8,6]{1,0:T(8,128)} %length_ref.1) | copy-start | bytes 580
  2.5 0.7 %copy-start.3 = (s32[8,6]{1,0:T(8,128)S(1)}, s32[8,6]{1,0:T(8,128)}, u32[]{:S(2)}) copy-start(s32[8,6]{1,0:T(8,128)} %map_ref.1) | copy-start | bytes 580
  2.5 0.7 %copy-start.4 = (s32[1,6]{1,0:T(1,128)S(1)}, s32[1,6]{1,0:T(1,128)}, u32[]{:S(2)}) copy-start(s32[1,6]{1,0:T(1,128)} %table_ref.1) | copy-start | bytes 76
  3.2 1.1 %copy-start = (bf16[1,6,4,2,64,128]{5,4,3,2,1,0:T(8,128)(2,1)S(1)}, bf16[1,6,4,2,64,128]{5,4,3,2,1,0:T(8,128)(2,1)}, u32[]{:S(2)}) copy-start(bf16[1,6,4,2,64,128]{5,4,3,2,1,0:T(8,128)(2,1)} %param.7) | copy-start | bytes 2359300

commit v2 on v1

--- a/solution.py
+++ b/solution.py
@@ -9,7 +9,6 @@
 from jax.sharding import PartitionSpec as P
 
 ROPE_BASE = 1000000.0
-HIGHEST = lax.Precision.HIGHEST
 MESH = pl.DeviceIdType.MESH
 F32 = jnp.float32
 BF16 = jnp.bfloat16
@@ -35,9 +34,9 @@
     return jnp.dot(a, b, preferred_element_type=F32)
 
 
-def dot_t(a, b, precision=None):
+def dot_t(a, b):
     return lax.dot_general(
-        a, b, (((1,), (1,)), ((), ())), precision=precision, preferred_element_type=F32
+        a, b, (((1,), (1,)), ((), ())), preferred_element_type=F32
     )
 
 
@@ -53,6 +52,7 @@
     out_ref,
     scale_ref,
     had,
+    own,
     other,
     quant,
     scale,
@@ -74,8 +74,8 @@
     me = lax.axis_index("inst")
     rank = lax.axis_index("tp")
     steps, _, requests, query_heads, width = query_ref.shape
-    heads = cache_ref.shape[1] // 2
-    half = cache_ref.shape[3]
+    heads = cache_ref.shape[2] // 2
+    half = cache_ref.shape[4]
     share = query_heads // heads
     rows = steps * share
     asks = heads * rows
@@ -87,6 +87,10 @@
     def before(d):
         return lax.rem(me + n - d, n)
 
+    fetch = pltpu.make_async_copy(
+        cache_ref.at[0, :, pl.ds(rank * heads, heads)], own, swap_sem.at[2]
+    )
+    fetch.start()
     barrier = pltpu.get_barrier_semaphore()
 
     pl.semaphore_signal(barrier, inc=1, device_id=(group, me, 1 - rank), device_id_type=MESH)
@@ -99,7 +103,7 @@
     pl.semaphore_wait(barrier, n)
 
     swap = pltpu.make_async_remote_copy(
-        src_ref=cache_ref.at[:, pl.ds((1 - rank) * heads, heads)],
+        src_ref=cache_ref.at[0, :, pl.ds((1 - rank) * heads, heads)],
         dst_ref=other,
         send_sem=swap_sem.at[0],
         recv_sem=swap_sem.at[1],
@@ -154,6 +158,7 @@
         turn_copy(d, me, source).start()
         ask_copy(d, me, source).start()
 
+    fetch.wait()
     swap.wait_recv()
 
     token = lax.broadcasted_iota(jnp.int32, (2 * half, width), 0)
@@ -169,7 +174,7 @@
         for g in range(heads):
             for e in range(2):
                 values = jnp.concatenate(
-                    [cache_ref[page, rank * heads + g, e], other[page, g, e]], axis=0
+                    [own[page, g, e], other[page, g, e]], axis=0
                 )
                 rotated = jnp.where(keep, dot(values, signs) * factor, 0.0)
                 top = jnp.max(jnp.max(jnp.abs(rotated), axis=0, keepdims=True), axis=1, keepdims=True)
@@ -179,17 +184,13 @@
         scale[j] = packed
 
     lane = lax.broadcasted_iota(jnp.int32, (8, width), 1)
-    row = lax.broadcasted_iota(jnp.int32, (rows, 8), 0)
-    later = lax.broadcasted_iota(jnp.int32, (rows, 8), 1)
+    row = lax.broadcasted_iota(jnp.int32, (rows, width), 0)
+    later = lax.broadcasted_iota(jnp.int32, (rows, width), 1)
     open_ = later * share <= row
     column = lax.broadcasted_iota(jnp.int32, (rows, 2 * half), 1)
     column = jnp.where(column < half, column + rank * half, column - half + (1 - rank) * half)
 
-    @pl.loop(1, n)
-    def _(d):
-        target = before(d)
-        turn_copy(d, target, target).wait_recv()
-        ask_copy(d, target, target).wait_recv()
+    def attend(target):
         chosen = jnp.int32(0)
         for j in range(requests):
             chosen = jnp.maximum(chosen, jnp.where(map_ref[me, j] == target, j, 0))
@@ -200,44 +201,62 @@
         flipped = pltpu.roll(turn, width // 2, 1)
         cosine = jnp.where(lane < width // 2, turn, flipped)
         sine = jnp.where(lane < width // 2, -flipped, turn)
-        wide_cosine = jnp.concatenate(
-            [jnp.broadcast_to(cosine[u : u + 1], (share, width)) for u in range(steps)], axis=0
-        )
-        wide_sine = jnp.concatenate(
-            [jnp.broadcast_to(sine[u : u + 1], (share, width)) for u in range(steps)], axis=0
-        )
+
+        def wide(values):
+            blocks = [jnp.broadcast_to(values[u : u + 1], (share, width)) for u in range(steps)]
+            return jnp.concatenate(blocks * heads, axis=0)
+
         fresh = asked[target, pl.ds(asks, 32), :].astype(F32)
+        query = asked[target, pl.ds(0, asks), :].astype(F32)
+        query = query * wide(cosine) + pltpu.roll(query, width // 2, 1) * wide(sine)
+        high, low = split(query)
+        query_high, query_low = split(dot(high, signs) + dot(low, signs))
+        zeros = jnp.zeros((8, width), F32)
+        blank = jnp.zeros((width - 16, width), BF16)
+        results = []
         for g in range(heads):
-            query = asked[target, pl.ds(g * rows, rows), :].astype(F32)
-            query = query * wide_cosine + pltpu.roll(query, width // 2, 1) * wide_sine
             key = fresh[16 * g : 16 * g + 8]
             key = key * cosine + pltpu.roll(key, width // 2, 1) * sine
-            value = fresh[16 * g + 8 : 16 * g + 16]
-            high, low = split(query)
-            mixed_high, mixed_low = split(dot(high, signs) + dot(low, signs))
-            keys = quant[chosen, g, 0]
-            cached = dot_t(mixed_high, keys) + dot_t(mixed_low, keys)
-            cached = cached * (packed[2 * g : 2 * g + 1] * (factor * factor))
+            high = key.astype(BF16).astype(F32)
+            key = dot(jnp.concatenate([high, key - high], axis=0).astype(BF16), signs)
+            key = key[:8] + key[8:]
+            high = key.astype(BF16).astype(F32)
+            key = jnp.concatenate([high, key - high], axis=0).astype(BF16)
+            keys = jnp.concatenate([quant[chosen, g, 0], key, blank], axis=0)
+            value = jnp.concatenate([fresh[16 * g + 8 : 16 * g + 16], zeros], axis=0).astype(BF16)
+            value = jnp.concatenate([signs, value, blank], axis=0)
+            mine = slice(g * rows, (g + 1) * rows)
+            scores = dot_t(query_high[mine], keys) + dot_t(query_low[mine], keys)
+            cached = scores[:, :width] * (packed[2 * g : 2 * g + 1] * (factor * factor))
             cached = jnp.where(keep, cached, -jnp.inf)
-            recent = dot_t(query, key, HIGHEST) * factor
+            recent = scores[:, width:]
+            recent = (recent + pltpu.roll(recent, width - 8, 1)) * (factor * factor * factor)
             recent = jnp.where(open_, recent, -jnp.inf)
-            top = jnp.maximum(
-                jnp.max(cached, axis=1, keepdims=True), jnp.max(recent, axis=1, keepdims=True)
-            )
-            cached = jnp.exp(cached - top)
-            recent = jnp.exp(recent - top)
-            total = jnp.sum(cached, axis=1, keepdims=True) + jnp.sum(recent, axis=1, keepdims=True)
-            high, low = split(cached)
-            values = quant[chosen, g, 1]
-            mixed = (dot(high, values) + dot(low, values)) * (
-                packed[2 * g + 1 : 2 * g + 2] * factor
-            )
-            high, low = split(mixed)
-            mixed = dot(high, signs) + dot(low, signs)
-            mixed = mixed + jnp.dot(recent, value, precision=HIGHEST, preferred_element_type=F32)
-            reply[target, pl.ds(g * rows, rows), :] = (mixed / total).astype(BF16)
-        reply[target, pl.ds(asks, 16), :] = packed.astype(BF16)
-        reply_copy(d, me, target).start()
+            top = jnp.max(jnp.maximum(cached, recent), axis=1, keepdims=True)
+            cached = jnp.exp(cached - top).astype(BF16)
+            recent = jnp.exp(recent - top).astype(BF16)
+            total = jnp.sum(cached.astype(F32) + recent.astype(F32), axis=1, keepdims=True)
+            mixed = dot(cached, quant[chosen, g, 1])
+            mixed = (mixed * (packed[2 * g + 1 : 2 * g + 2] * factor)).astype(BF16)
+            mixed = dot(jnp.concatenate([mixed, recent], axis=1), value)
+            results.append((mixed / total).astype(BF16))
+        results.append(packed.astype(BF16))
+        return jnp.concatenate(results, axis=0)
+
+    def serve(distances):
+        for d in distances:
+            turn_copy(d, before(d), before(d)).wait_recv()
+            ask_copy(d, before(d), before(d)).wait_recv()
+        results = [attend(before(d)) for d in distances]
+        for d, result in zip(distances, results):
+            reply[before(d)] = result
+            reply_copy(d, me, before(d)).start()
+
+    serve([1])
+
+    @pl.loop(0, (n - 2) // 2)
+    def _(pair):
+        serve([2 + 2 * pair, 3 + 2 * pair])
 
     @pl.loop(1, n)
     def _(d):
@@ -288,10 +307,11 @@
             jax.ShapeDtypeStruct(queries.shape, BF16),
             jax.ShapeDtypeStruct((requests, 16, width), BF16),
         ),
-        in_specs=[smem] * 3 + [vmem] * 4,
+        in_specs=[smem] * 3 + [pl.BlockSpec(memory_space=pl.ANY)] + [vmem] * 3,
         out_specs=(vmem, vmem),
         scratch_shapes=[
             pltpu.VMEM((width, width), BF16),
+            pltpu.VMEM((requests, heads, pair, half, width), BF16),
             pltpu.VMEM((requests, heads, pair, half, width), BF16),
             pltpu.VMEM((requests, heads, pair, 2 * half, width), BF16),
             pltpu.VMEM((requests, 16, width), F32),
@@ -301,7 +321,7 @@
             pltpu.VMEM((n, 8, width), F32),
             pltpu.VMEM((n, asks + 16, width), BF16),
             pltpu.VMEM((n, asks + 16, width), BF16),
-            dma((2,)),
+            dma((3,)),
             dma((n,)),
             dma((n,)),
             dma((n,)),
@@ -313,7 +333,7 @@
             collective_id=0, has_side_effects=True, vmem_limit_bytes=52 * 2**20
         ),
         cost_estimate=pl.CostEstimate(flops=10**9, bytes_accessed=4 * 10**6, transcendentals=10**5),
-    )(block_table, lengths, target_map, source_cache[0], queries, fresh, turn)
+    )(block_table, lengths, target_map, source_cache, queries, fresh, turn)
     scales = scales[:, : heads * pair, 0].reshape(1, requests, heads, pair)
     return scales, attended
 

time: 40.4 us -> 41.6 us (1.030)
  Pallas kernels: 34.4 us -> 35.6 us
    pallas_call x1, Pallas kernels: 34.4 us -> 35.6 us  [on_device(): pl.pallas_call(functools.partial(kernel, n), out_shape=(jax.ShapeDtypeStr...]
where the time goes in v2:
time: 41.6 us; the launch traced here: 41.3 us
  Pallas kernels  35.6 us (86%)
  local copies, waits for them, and re-layouts  3.99 us (10%)
  other arithmetic  1.02 us (2%)
  between operations  0.71 us (2%)
    pallas_call x1, Pallas kernels, on_device(): pl.pallas_call(functools.partial(kernel, n), out_shape=(jax.ShapeDtypeStr...  35.6 us
    unnamed x12, local copies, waits for them, and re-layouts  3.29 us

profile of v2, /device:TPU:0, one launch (start us, length us, event | category | flops | bytes accessed | tf_op | source)
XLA Modules:
  0.0 41.3 jit_solution(8337253062037434306)
XLA Ops:
  0.6 0.0 copy-start.1
  0.7 0.8 %add_convert_fusion = f32[6,8]{1,0:T(8,128)S(1)} fusion(s32[6]{0:T(128)} %bitcast.9), kind=kLoop, calls=%fused_computation.3 | loop fusion | flops 96 | bytes 216 | tf_op jit(solution)/shard_map/convert_element_type | solution.py:296
  1.4 0.2 multiply_cosine_fusion
  1.6 0.1 pad_maximum_fusion.turn_ref
  1.7 0.8 %copy.11 = bf16[6,2,2,6,128]{4,3,2,1,0:T(8,128)(2,1)S(1)} copy(bf16[6,2,2,6,128]{4,2,1,0,3:T(2,128)(2,1)} %bitcast.7) | data formatting | bytes 73728
  2.5 0.0 copy-start.2
  2.5 0.0 copy-start.3
  2.5 0.0 copy-start.4
  2.5 0.0 copy-done.1
  2.5 0.6 %copy-done.2 = s32[8,6]{1,0:T(8,128)S(1)} copy-done((s32[8,6]{1,0:T(8,128)S(1)}, s32[8,6]{1,0:T(8,128)}, u32[]{:S(2)}) %copy-start.2) | copy-done | bytes 216
  3.2 0.0 copy-done.3
  3.2 0.0 copy-done.4
  3.2 0.0 copy-start
  3.2 1.1 %copy-done = bf16[1,6,4,2,64,128]{5,4,3,2,1,0:T(8,128)(2,1)S(1)} copy-done((bf16[1,6,4,2,64,128]{5,4,3,2,1,0:T(8,128)(2,1)S(1)}, bf16[1,6,4,2,64,128]{5,4,3,2,1,0:T(8,128)(2,1)}, u32[]{:S(2)}) %copy-start) | copy-done | bytes 786456
  4.3 35.6 %shard_map.86 = (bf16[6,1,6,32,128]{4,3,2,1,0:T(8,128)(2,1)S(1)}, bf16[6,16,128]{2,1,0:T(8,128)(2,1)S(1)}) custom-call(s32[1,6]{1,0:T(1,128)S(1)} %copy-done.4, s32[8,6]{1,0:T(8,128)S(1)} %copy-done.2, s32[8,6]{1,0:T(8,128)S(1)} %copy-done.3, bf16[1,6,4,2,64,128]{5,4,3,2,1,0:T(8,128)(2,1)S(1)} %copy-done, bf16[6,1,6,32,128]{4,3,2,1,0:T(8,128)(2,1)S(1)} %copy-done.1, ...), custom_call_target="tpu_custom_call" | custom-call | flops 1000000000 | bytes 4000000 | tf_op jit(solution)/shard_map/pallas_call | solution.py:304
  39.9 0.7 %copy.10 = bf16[6,4,1]{0,1,2:T(4,128)(2,1)} copy(bf16[6,4,1]{2,1,0:T(4,128)(2,1)S(1)} %slice.3) | data formatting | bytes 96 | tf_op jit(solution)/shard_map/slice | solution.py:337
  40.6 0.7 %copy.13 = bf16[6,1,6,32,128]{4,3,2,1,0:T(8,128)(2,1)} copy(bf16[6,1,6,32,128]{4,3,2,1,0:T(8,128)(2,1)S(1)} %get-tuple-element.11) | data formatting | bytes 589824
  (3 shorter events, 0.0 us)
Async XLA Ops:
  0.6 1.9 %copy-start.1 = (bf16[6,1,6,32,128]{4,3,2,1,0:T(8,128)(2,1)S(1)}, bf16[6,1,6,32,128]{4,3,2,1,0:T(8,128)(2,1)}, u32[]{:S(2)}) copy-start(bf16[6,1,6,32,128]{4,3,2,1,0:T(8,128)(2,1)} %query_ref.1) | copy-start | bytes 884740
  2.5 0.7 %copy-start.2 = (s32[8,6]{1,0:T(8,128)S(1)}, s32[8,6]{1,0:T(8,128)}, u32[]{:S(2)}) copy-start(s32[8,6]{1,0:T(8,128)} %length_ref.1) | copy-start | bytes 580
  2.5 0.7 %copy-start.3 = (s32[8,6]{1,0:T(8,128)S(1)}, s32[8,6]{1,0:T(8,128)}, u32[]{:S(2)}) copy-start(s32[8,6]{1,0:T(8,128)} %map_ref.1) | copy-start | bytes 580
  2.5 0.7 %copy-start.4 = (s32[1,6]{1,0:T(1,128)S(1)}, s32[1,6]{1,0:T(1,128)}, u32[]{:S(2)}) copy-start(s32[1,6]{1,0:T(1,128)} %table_ref.1) | copy-start | bytes 76
  3.2 1.1 %copy-start = (bf16[1,6,4,2,64,128]{5,4,3,2,1,0:T(8,128)(2,1)S(1)}, bf16[1,6,4,2,64,128]{5,4,3,2,1,0:T(8,128)(2,1)}, u32[]{:S(2)}) copy-start(bf16[1,6,4,2,64,128]{5,4,3,2,1,0:T(8,128)(2,1)} %cache_ref.1) | copy-start | bytes 2359300

commit v3 on v2

--- a/solution.py
+++ b/solution.py
@@ -42,15 +42,19 @@
 
 def kernel(
     n,
-    table_ref,
-    length_ref,
-    map_ref,
+    table_hbm,
+    length_hbm,
+    map_hbm,
     cache_ref,
-    query_ref,
+    query_hbm,
     fresh_ref,
     turn_ref,
     out_ref,
     scale_ref,
+    table_ref,
+    length_ref,
+    map_ref,
+    query_ref,
     had,
     own,
     other,
@@ -91,6 +95,14 @@
         cache_ref.at[0, :, pl.ds(rank * heads, heads)], own, swap_sem.at[2]
     )
     fetch.start()
+    plans = [
+        pltpu.make_async_copy(map_hbm, map_ref, swap_sem.at[3]),
+        pltpu.make_async_copy(table_hbm, table_ref, swap_sem.at[4]),
+        pltpu.make_async_copy(length_hbm, length_ref, swap_sem.at[5]),
+        pltpu.make_async_copy(query_hbm, query_ref, swap_sem.at[6]),
+    ]
+    for plan in plans:
+        plan.start()
     barrier = pltpu.get_barrier_semaphore()
 
     pl.semaphore_signal(barrier, inc=1, device_id=(group, me, 1 - rank), device_id_type=MESH)
@@ -100,47 +112,8 @@
         pl.semaphore_signal(barrier, inc=1, device_id=(group, after(d), rank), device_id_type=MESH)
 
     had[...] = sylvester(width)
-    pl.semaphore_wait(barrier, n)
-
-    swap = pltpu.make_async_remote_copy(
-        src_ref=cache_ref.at[0, :, pl.ds((1 - rank) * heads, heads)],
-        dst_ref=other,
-        send_sem=swap_sem.at[0],
-        recv_sem=swap_sem.at[1],
-        device_id=(group, me, 1 - rank),
-        device_id_type=MESH,
-    )
-    swap.start()
-
-    def ask_copy(d, slot, target):
-        return pltpu.make_async_remote_copy(
-            src_ref=ask.at[after(d)],
-            dst_ref=asked.at[slot],
-            send_sem=ask_send.at[d],
-            recv_sem=ask_recv.at[d],
-            device_id=(group, target, rank),
-            device_id_type=MESH,
-        )
-
-    def turn_copy(d, slot, target):
-        return pltpu.make_async_remote_copy(
-            src_ref=turns.at[after(d)],
-            dst_ref=turned.at[slot],
-            send_sem=turn_send.at[d],
-            recv_sem=turn_recv.at[d],
-            device_id=(group, target, rank),
-            device_id_type=MESH,
-        )
-
-    def reply_copy(d, slot, target):
-        return pltpu.make_async_remote_copy(
-            src_ref=reply.at[before(d)],
-            dst_ref=replied.at[slot],
-            send_sem=reply_send.at[d],
-            recv_sem=reply_recv.at[d],
-            device_id=(group, target, rank),
-            device_id_type=MESH,
-        )
+    plans[0].wait()
+    plans[3].wait()
 
     @pl.loop(1, n)
     def _(d):
@@ -155,10 +128,58 @@
                 ]
         ask[source, pl.ds(asks, 32), :] = fresh_ref[chosen]
         turns[source] = turn_ref[chosen]
+
+    pl.semaphore_wait(barrier, n)
+
+    swap = pltpu.make_async_remote_copy(
+        src_ref=cache_ref.at[0, :, pl.ds((1 - rank) * heads, heads)],
+        dst_ref=other,
+        send_sem=swap_sem.at[0],
+        recv_sem=swap_sem.at[1],
+        device_id=(group, me, 1 - rank),
+        device_id_type=MESH,
+    )
+    swap.start()
+
+    def ask_copy(d, slot, target):
+        return pltpu.make_async_remote_copy(
+            src_ref=ask.at[after(d)],
+            dst_ref=asked.at[slot],
+            send_sem=ask_send.at[d],
+            recv_sem=ask_recv.at[d],
+            device_id=(group, target, rank),
+            device_id_type=MESH,
+        )
+
+    def turn_copy(d, slot, target):
+        return pltpu.make_async_remote_copy(
+            src_ref=turns.at[after(d)],
+            dst_ref=turned.at[slot],
+            send_sem=turn_send.at[d],
+            recv_sem=turn_recv.at[d],
+            device_id=(group, target, rank),
+            device_id_type=MESH,
+        )
+
+    def reply_copy(d, slot, target):
+        return pltpu.make_async_remote_copy(
+            src_ref=reply.at[before(d)],
+            dst_ref=replied.at[slot],
+            send_sem=reply_send.at[d],
+            recv_sem=reply_recv.at[d],
+            device_id=(group, target, rank),
+            device_id_type=MESH,
+        )
+
+    @pl.loop(1, n)
+    def _(d):
+        source = after(d)
         turn_copy(d, me, source).start()
         ask_copy(d, me, source).start()
 
     fetch.wait()
+    plans[1].wait()
+    plans[2].wait()
     swap.wait_recv()
 
     token = lax.broadcasted_iota(jnp.int32, (2 * half, width), 0)
@@ -252,11 +273,9 @@
             reply[before(d)] = result
             reply_copy(d, me, before(d)).start()
 
-    serve([1])
-
-    @pl.loop(0, (n - 2) // 2)
-    def _(pair):
-        serve([2 + 2 * pair, 3 + 2 * pair])
+    @pl.loop(1, n)
+    def _(d):
+        serve([d])
 
     @pl.loop(1, n)
     def _(d):
@@ -298,7 +317,7 @@
     fresh = jnp.transpose(fresh_cache[:, 0], (1, 2, 3, 0, 4))
     fresh = jnp.pad(fresh, ((0, 0), (0, 0), (0, 0), (0, 8 - steps), (0, 0)))
     fresh = fresh.reshape(requests, heads * pair * 8, width)
-    smem = pl.BlockSpec(memory_space=pltpu.SMEM)
+    hbm = pl.BlockSpec(memory_space=pltpu.HBM)
     vmem = pl.BlockSpec(memory_space=pltpu.VMEM)
     dma = pltpu.SemaphoreType.DMA
     attended, scales = pl.pallas_call(
@@ -307,9 +326,13 @@
             jax.ShapeDtypeStruct(queries.shape, BF16),
             jax.ShapeDtypeStruct((requests, 16, width), BF16),
         ),
-        in_specs=[smem] * 3 + [pl.BlockSpec(memory_space=pl.ANY)] + [vmem] * 3,
+        in_specs=[hbm] * 5 + [vmem] * 2,
         out_specs=(vmem, vmem),
         scratch_shapes=[
+            pltpu.SMEM(block_table.shape, jnp.int32),
+            pltpu.SMEM(lengths.shape, jnp.int32),
+            pltpu.SMEM(target_map.shape, jnp.int32),
+            pltpu.VMEM(queries.shape, BF16),
             pltpu.VMEM((width, width), BF16),
             pltpu.VMEM((requests, heads, pair, half, width), BF16),
             pltpu.VMEM((requests, heads, pair, half, width), BF16),
@@ -321,7 +344,7 @@
             pltpu.VMEM((n, 8, width), F32),
             pltpu.VMEM((n, asks + 16, width), BF16),
             pltpu.VMEM((n, asks + 16, width), BF16),
-            dma((3,)),
+            dma((7,)),
             dma((n,)),
             dma((n,)),
             dma((n,)),
@@ -330,7 +353,7 @@
             dma((n,)),
         ],
         compiler_params=pltpu.CompilerParams(
-            collective_id=0, has_side_effects=True, vmem_limit_bytes=52 * 2**20
+            collective_id=0, has_side_effects=True, vmem_limit_bytes=61 * 2**20
         ),
         cost_estimate=pl.CostEstimate(flops=10**9, bytes_accessed=4 * 10**6, transcendentals=10**5),
     )(block_table, lengths, target_map, source_cache, queries, fresh, turn)

time: 41.6 us -> 41.9 us (level)
  local copies, waits for them, and re-layouts: 3.99 us -> 4.44 us
    unnamed x12 -> x6, local copies, waits for them, and re-layouts: 3.29 us -> 2.42 us
    slice x2, local copies, waits for them, and re-layouts: 0.69 us -> 1.39 us  [on_device(): scales = scales[:, :heads * pair, 0].reshape(1, requests, heads, pair)]
    convert_element_type x1, other arithmetic: 0.77 us -> 0.07 us  [on_device(): angles = places.astype(F32)[..., None] * frequency]
    pad x1, local copies, waits for them, and re-layouts: 0.01 us -> 0.63 us  [on_device(): fresh = jnp.pad(fresh, ((0, 0), (0, 0), (0, 0), (0, 8 - steps), (0, 0)))]
    concatenate x1, other arithmetic: 0.08 us -> 0.68 us  [on_device(): turn = jnp.concatenate([jnp.cos(angles), jnp.sin(angles)], axis=-1)]
where the time goes in v3:
time: 41.9 us; the launch traced here: 41.5 us
  Pallas kernels  35.5 us (85%)
  local copies, waits for them, and re-layouts  4.44 us (11%)
  other arithmetic  0.93 us (2%)
  between operations  0.67 us (2%)
    pallas_call x1, Pallas kernels, on_device(): pl.pallas_call(functools.partial(kernel, n), out_shape=(jax.ShapeDtypeStr...  35.5 us
    unnamed x6, local copies, waits for them, and re-layouts  2.42 us
    slice x2, local copies, waits for them, and re-layouts, on_device(): scales = scales[:, :heads * pair, 0].reshape(1, requests, heads, pair)  1.39 us

profile of v3, /device:TPU:0, one launch (start us, length us, event | category | flops | bytes accessed | tf_op | source)
XLA Modules:
  0.0 41.5 jit_solution(9788763878961484668)
XLA Ops:
  0.6 0.0 copy-start.1
  0.7 0.6 %copy-done.1 = s32[1,6]{1,0:T(1,128)S(1)} copy-done((s32[1,6]{1,0:T(1,128)S(1)}, s32[1,6]{1,0:T(1,128)}, u32[]{:S(2)}) %copy-start.1) | copy-done | bytes 48
  1.3 0.1 add_convert_fusion
  1.4 0.2 multiply_cosine_fusion
  1.5 0.0 copy-start
  1.5 0.7 %pad_maximum_fusion.turn_ref = f32[6,8,128]{2,1,0:T(8,128)} fusion(f32[6,8,64]{2,1,0:T(8,128)S(1)} %get-tuple-element.7, f32[6,8,64]{2,1,0:T(8,128)S(1)} %get-tuple-element.6), kind=kLoop, calls=%fused_computation.2 | loop fusion | flops 6144 | bytes 49152 | tf_op jit(solution)/shard_map/concatenate | solution.py:316
  2.2 0.1 copy-done
  2.3 0.6 %pad.4.clone = bf16[6,2,2,8,128]{4,3,2,1,0:T(8,128)(2,1)} pad(bf16[6,2,2,6,128]{4,3,2,1,0:T(8,128)(2,1)S(1)} %copy.11, bf16[]{:T(256)} %constant.1.clone.1), padding=0_0x0_0x0_0x0_2x0_0 | pad | bytes 86018 | tf_op jit(solution)/shard_map/jit(_pad)/pad | solution.py:318
  3.0 35.5 %shard_map.86 = (bf16[6,1,6,32,128]{4,3,2,1,0:T(8,128)(2,1)}, bf16[6,16,128]{2,1,0:T(8,128)(2,1)}) custom-call(s32[1,6]{1,0:T(1,128)} %table_hbm.1, s32[8,6]{1,0:T(8,128)} %length_hbm.1, s32[8,6]{1,0:T(8,128)} %map_hbm.1, bf16[1,6,4,2,64,128]{5,4,3,2,1,0:T(8,128)(2,1)} %cache_ref.1, bf16[6,1,6,32,128]{4,3,2,1,0:T(8,128)(2,1)} %query_hbm.1, ...), custom_call_target="tpu_custom_call" | custom-call | flops 1000000000 | bytes 4000000 | tf_op jit(solution)/shard_map/pallas_call | solution.py:323
  38.4 0.7 %slice.3 = bf16[6,4,1]{2,1,0:T(4,128)(2,1)S(1)} slice(bf16[6,16,128]{2,1,0:T(8,128)(2,1)} %get-tuple-element.4), slice={[0:6], [0:4], [0:1]} | slice | bytes 96 | tf_op jit(solution)/shard_map/slice | solution.py:360
  39.1 0.7 %copy.10 = bf16[6,4,1]{0,1,2:T(4,128)(2,1)} copy(bf16[6,4,1]{2,1,0:T(4,128)(2,1)S(1)} %slice.3) | data formatting | bytes 96 | tf_op jit(solution)/shard_map/slice | solution.py:360
  39.8 1.7 %copy.13 = bf16[6,1,6,32,128]{4,3,2,1,0:T(8,128)(2,1)} copy(bf16[6,1,6,32,128]{4,3,2,1,0:T(8,128)(2,1)} %get-tuple-element.11) | data formatting | bytes 589824
  (2 shorter events, 0.0 us)
Async XLA Ops:
  0.6 0.7 %copy-start.1 = (s32[1,6]{1,0:T(1,128)S(1)}, s32[1,6]{1,0:T(1,128)}, u32[]{:S(2)}) copy-start(s32[1,6]{1,0:T(1,128)} %param.13) | copy-start | bytes 76
  1.5 0.8 %copy-start = (bf16[6,1,6,2,2,128]{5,4,3,2,1,0:T(2,128)(2,1)S(1)}, bf16[6,1,6,2,2,128]{5,4,3,2,1,0:T(2,128)(2,1)}, u32[]{:S(2)}) copy-start(bf16[6,1,6,2,2,128]{5,4,3,2,1,0:T(2,128)(2,1)} %param.12) | copy-start | bytes 110596

commit v4 on v3

--- a/solution.py
+++ b/solution.py
@@ -273,9 +273,11 @@
             reply[before(d)] = result
             reply_copy(d, me, before(d)).start()
 
-    @pl.loop(1, n)
-    def _(d):
-        serve([d])
+    serve([1])
+
+    @pl.loop(0, (n - 2) // 2)
+    def _(pair):
+        serve([2 + 2 * pair, 3 + 2 * pair])
 
     @pl.loop(1, n)
     def _(d):
@@ -353,7 +355,7 @@
             dma((n,)),
         ],
         compiler_params=pltpu.CompilerParams(
-            collective_id=0, has_side_effects=True, vmem_limit_bytes=61 * 2**20
+            collective_id=0, has_side_effects=True, vmem_limit_bytes=53 * 2**20
         ),
         cost_estimate=pl.CostEstimate(flops=10**9, bytes_accessed=4 * 10**6, transcendentals=10**5),
     )(block_table, lengths, target_map, source_cache, queries, fresh, turn)

time: 41.9 us -> 39.8 us (0.950)
  local copies, waits for them, and re-layouts: 4.44 us -> 2.85 us
  Pallas kernels: 35.5 us -> 35 us
    slice x2, local copies, waits for them, and re-layouts: 1.39 us -> 0.69 us  [on_device(): scales = scales[:, :heads * pair, 0].reshape(1, requests, heads, pair)]
    convert_element_type x1, other arithmetic: 0.07 us -> 0.77 us  [on_device(): angles = places.astype(F32)[..., None] * frequency]
    pad x1, local copies, waits for them, and re-layouts: 0.63 us -> 0.01 us  [on_device(): fresh = jnp.pad(fresh, ((0, 0), (0, 0), (0, 0), (0, 8 - steps), (0, 0)))]
    concatenate x1, other arithmetic: 0.68 us -> 0.08 us  [on_device(): turn = jnp.concatenate([jnp.cos(angles), jnp.sin(angles)], axis=-1)]
    pallas_call x1, Pallas kernels: 35.5 us -> 35 us  [on_device(): pl.pallas_call(functools.partial(kernel, n), out_shape=(jax.ShapeDtypeStr...]
    unnamed x6 -> x10, local copies, waits for them, and re-layouts: 2.42 us -> 2.15 us
where the time goes in v4:
time: 39.8 us; the launch traced here: 39.6 us
  Pallas kernels  35 us (88%)
  local copies, waits for them, and re-layouts  2.85 us (7%)
  other arithmetic  1.02 us (3%)
  between operations  0.71 us (2%)
    pallas_call x1, Pallas kernels, on_device(): pl.pallas_call(functools.partial(kernel, n), out_shape=(jax.ShapeDtypeStr...  35 us
    unnamed x10, local copies, waits for them, and re-layouts  2.15 us

profile of v4, /device:TPU:0, one launch (start us, length us, event | category | flops | bytes accessed | tf_op | source)
XLA Modules:
  0.0 39.6 jit_solution(13472485286857213475)
XLA Ops:
  0.6 0.0 copy-start
  0.7 0.8 %add_convert_fusion = f32[6,8]{1,0:T(8,128)S(1)} fusion(s32[6]{0:T(128)} %bitcast.9), kind=kLoop, calls=%fused_computation.3 | loop fusion | flops 96 | bytes 216 | tf_op jit(solution)/shard_map/convert_element_type | solution.py:317
  1.4 0.2 multiply_cosine_fusion
  1.6 0.1 pad_maximum_fusion.turn_ref
  1.7 0.8 %copy.11 = bf16[6,2,2,6,128]{4,3,2,1,0:T(8,128)(2,1)S(1)} copy(bf16[6,2,2,6,128]{4,2,1,0,3:T(2,128)(2,1)} %bitcast.7) | data formatting | bytes 73728
  2.5 0.0 copy-start.1
  2.5 0.0 copy-start.2
  2.5 0.0 copy-start.3
  2.5 0.0 copy-done
  2.5 0.6 %copy-done.1 = s32[8,6]{1,0:T(8,128)S(1)} copy-done((s32[8,6]{1,0:T(8,128)S(1)}, s32[8,6]{1,0:T(8,128)}, u32[]{:S(2)}) %copy-start.1) | copy-done | bytes 216
  3.2 0.0 copy-done.2
  3.2 0.0 copy-done.3
  3.2 35.0 %shard_map.86 = (bf16[6,1,6,32,128]{4,3,2,1,0:T(8,128)(2,1)S(1)}, bf16[6,16,128]{2,1,0:T(8,128)(2,1)S(1)}) custom-call(s32[1,6]{1,0:T(1,128)S(1)} %copy-done.3, s32[8,6]{1,0:T(8,128)S(1)} %copy-done.1, s32[8,6]{1,0:T(8,128)S(1)} %copy-done.2, bf16[1,6,4,2,64,128]{5,4,3,2,1,0:T(8,128)(2,1)} %cache_ref.1, bf16[6,1,6,32,128]{4,3,2,1,0:T(8,128)(2,1)S(1)} %copy-done, ...), custom_call_target="tpu_custom_call" | custom-call | flops 1000000000 | bytes 4000000 | tf_op jit(solution)/shard_map/pallas_call | solution.py:325
  38.2 0.7 %copy.10 = bf16[6,4,1]{0,1,2:T(4,128)(2,1)} copy(bf16[6,4,1]{2,1,0:T(4,128)(2,1)S(1)} %slice.3) | data formatting | bytes 96 | tf_op jit(solution)/shard_map/slice | solution.py:362
  38.8 0.7 %copy.13 = bf16[6,1,6,32,128]{4,3,2,1,0:T(8,128)(2,1)} copy(bf16[6,1,6,32,128]{4,3,2,1,0:T(8,128)(2,1)S(1)} %get-tuple-element.11) | data formatting | bytes 589824
  (3 shorter events, 0.0 us)
Async XLA Ops:
  0.6 1.9 %copy-start = (bf16[6,1,6,32,128]{4,3,2,1,0:T(8,128)(2,1)S(1)}, bf16[6,1,6,32,128]{4,3,2,1,0:T(8,128)(2,1)}, u32[]{:S(2)}) copy-start(bf16[6,1,6,32,128]{4,3,2,1,0:T(8,128)(2,1)} %query_hbm.1) | copy-start | bytes 884740
  2.5 0.7 %copy-start.1 = (s32[8,6]{1,0:T(8,128)S(1)}, s32[8,6]{1,0:T(8,128)}, u32[]{:S(2)}) copy-start(s32[8,6]{1,0:T(8,128)} %length_hbm.1) | copy-start | bytes 580
  2.5 0.7 %copy-start.2 = (s32[8,6]{1,0:T(8,128)S(1)}, s32[8,6]{1,0:T(8,128)}, u32[]{:S(2)}) copy-start(s32[8,6]{1,0:T(8,128)} %map_hbm.1) | copy-start | bytes 580
  2.5 0.7 %copy-start.3 = (s32[1,6]{1,0:T(1,128)S(1)}, s32[1,6]{1,0:T(1,128)}, u32[]{:S(2)}) copy-start(s32[1,6]{1,0:T(1,128)} %table_hbm.1) | copy-start | bytes 76
